TPU v7x, 512 devices: a whole 4x8x8 slice. The times are simulated.
512 devices in a mesh: sec: 4 (over x), tile: 128 (over y, z, core).
Axes of the slice: x: 4, y: 8, z: 8, core: 2. Of those that a mesh axis runs over, the one named last changes fastest.
Arguments:
- pre_act: bfloat16 [4, 131072, 512], P('sec', 'tile'), may hold values from -6 to 6
- edge_cot: bfloat16 [4, 131072, 512], P('sec', 'tile'), may hold values from -4 to 4
- recv_local: int32 [4, 131072], P('sec', 'tile'), may hold values from 0 to 127
- send_slot: int32 [4, 131072], P('sec', 'tile'), may hold values from 0 to 639
- edge_count: int32 [4, 128], P('sec', 'tile'), may hold values from 256 to 1024, as said below
- halo_map: int32 [4, 128, 128], P('sec', 'tile'), may hold values from 0 to 511
- dec_rows: bfloat16 [4, 65536, 512], P('sec', 'tile'), may hold values from -4 to 4
- dec_count: int32 [4, 1024], P('sec', 'tile'), may hold values from 1 to 64, as said below
- dec_node: int32 [4, 65536], P('sec', 'tile'), may hold values from 0 to 127, as said below
- w_node: bfloat16 [1024, 512], replicated, may hold values from -0.15625 to 0.15625
- w_out: bfloat16 [512, 512], replicated, may hold values from -0.25 to 0.25
Outputs:
- node_grad: float32 [4, 16384, 512], P('sec', 'tile')
Inputs may be any that keep to these rules, and one draw needn't show every extreme that they name: `edge_count`: some device has all 1024 edge slots live. `dec_count`: in each block q one offset has 64 live rows from every source tile. `dec_node`: rows c and c2 of one destination and offset with c // 4 == c2 // 4 name the same node.
All inputs are finite; a program needn't handle non-finite values.
Results may differ from a plain program's by a relative error of at most 0.0035.
Values may be sent and summed in bfloat16 or wider, within the bound.
A program may use at most 64 MiB of HBM per device.

v0:
```python
import jax
import jax.numpy as jnp
from jax import lax
from jax.sharding import PartitionSpec as P

QUART = 128


def from_behind(block, axis, distance):
    devices = range(lax.axis_size(axis))
    route = [((i - distance) % len(devices), i) for i in devices]
    return lax.ppermute(block, axis, route)


def offset_value(number, neighbours):
    half = neighbours // 2
    if number >= half:
        return number - half + 1
    return number - half


def per_device(
    pre_act,
    edge_cot,
    recv_local,
    send_slot,
    edge_count,
    halo_map,
    dec_rows,
    dec_count,
    dec_node,
    w_node,
    w_out,
):
    sec_count = lax.axis_size("sec")
    latent = pre_act.shape[2]
    edge_total = pre_act.shape[1]
    neighbours = dec_count.shape[1]
    capacity = dec_rows.shape[1] // neighbours
    halo_width = halo_map.shape[2] // neighbours
    dec_block = dec_rows[0].reshape(neighbours, capacity, latent)
    live_mask = lax.broadcasted_iota(jnp.int32, (neighbours, capacity), 1) < dec_count[0][:, None]
    dec_block = jnp.where(live_mask[:, :, None], dec_block, jnp.zeros_like(dec_block))
    node_table = dec_node[0].reshape(neighbours, capacity)
    pieces = []
    for number in range(neighbours):
        pieces.append(from_behind(dec_block[number], "tile", offset_value(number, neighbours)))
    arrived_flat = jnp.concatenate(pieces, axis=0)
    target = node_table.reshape(neighbours * capacity)
    one_hot = (
        target[None, :] == lax.broadcasted_iota(jnp.int32, (QUART, target.shape[0]), 0)
    ).astype(jnp.bfloat16)
    node_cot = jnp.dot(one_hot, arrived_flat, preferred_element_type=jnp.float32)
    node_low = node_cot.astype(jnp.bfloat16)
    contract_last = (((1,), (1,)), ((), ()))
    edge_proj = lax.dot_general(
        edge_cot[0], w_out, contract_last, preferred_element_type=jnp.float32
    )
    node_proj = lax.dot_general(node_low, w_out, contract_last, preferred_element_type=jnp.float32)
    delta_act = jnp.take(node_proj, recv_local[0], axis=0) + edge_proj
    preact = pre_act[0].astype(jnp.float32)
    logistic = jax.nn.sigmoid(preact)
    slope_act = logistic * (1.0 + preact * (1.0 - logistic))
    edge_live = lax.broadcasted_iota(jnp.int32, (edge_total, 1), 0) < edge_count[0, 0]
    delta_pre = jnp.where(edge_live, delta_act * slope_act, jnp.float32(0.0)).astype(jnp.bfloat16)
    delta_in = lax.dot_general(delta_pre, w_node, contract_last, preferred_element_type=jnp.float32)
    grad_send = delta_in[:, :latent].astype(jnp.bfloat16)
    grad_recv = delta_in[:, latent:].astype(jnp.bfloat16)
    recv_hot = (
        recv_local[0][None, :] == lax.broadcasted_iota(jnp.int32, (QUART, edge_total), 0)
    ).astype(jnp.bfloat16)
    recv_total = jnp.dot(recv_hot, grad_recv, preferred_element_type=jnp.float32)
    local_rows = sec_count * QUART
    slots = send_slot[0]
    halo_cols = local_rows + lax.broadcasted_iota(
        jnp.int32, (neighbours * halo_width, edge_total), 0
    )
    halo_hot_send = (slots[None, :] == halo_cols).astype(jnp.bfloat16)
    halo_total = jnp.dot(halo_hot_send, grad_send, preferred_element_type=jnp.float32)
    halo_out = halo_total.reshape(neighbours, halo_width, latent)
    landed_pieces = []
    for number in range(neighbours):
        landed_pieces.append(
            from_behind(halo_out[number], "tile", offset_value(number, neighbours))
        )
    halo_in = jnp.concatenate(landed_pieces, axis=0)
    halo_hot = (
        halo_map[0, 0][None, :]
        == lax.broadcasted_iota(jnp.int32, (local_rows, neighbours * halo_width), 0)
    ).astype(jnp.float32)
    landed = jnp.dot(
        halo_hot, halo_in, precision=lax.Precision.HIGHEST, preferred_element_type=jnp.float32
    )
    send_hot = (
        slots[None, :] == lax.broadcasted_iota(jnp.int32, (local_rows, edge_total), 0)
    ).astype(jnp.bfloat16)
    send_total = jnp.dot(send_hot, grad_send, preferred_element_type=jnp.float32)
    own_quarter = lax.psum_scatter(send_total + landed, "sec", scatter_dimension=0, tiled=True)
    return (node_cot + recv_total + own_quarter)[None]


def solution(mesh):
    return jax.shard_map(
        per_device,
        mesh=mesh,
        in_specs=(
            P("sec", "tile", None),
            P("sec", "tile", None),
            P("sec", "tile"),
            P("sec", "tile"),
            P("sec", "tile"),
            P("sec", "tile", None),
            P("sec", "tile", None),
            P("sec", "tile"),
            P("sec", "tile"),
            P(),
            P(),
        ),
        out_specs=P("sec", "tile", None),
        check_vma=False,
    )
```

profile of v0, /device:TPU:1, one launch (start us, length us, event | category | flops | bytes accessed | tf_op | source)
XLA Modules:
  0.0 128.2 jit_solution(13470899514400410159)
XLA Ops:
  6.5 0.0 reduce-scatter.2.cloned.1.call-start
  6.6 0.8 iota_compare_fusion.9
  7.4 1.2 broadcast_select_fusion
  8.7 14.4 %collective-permute-start = (bf16[64,512]{1,0:T(8,128)(2,1)S(1)}, bf16[64,512]{1,0:T(8,128)(2,1)S(1)}, u32[]{:S(2)}, u32[]{:S(2)}) collective-permute-start(bf16[64,512]{1,0:T(8,128)(2,1)S(1)} %get-tuple-element.12), channel_id=1, source_target_pairs={{4,0},{5,1},{6,2},{7,3},{8,4},{9,5},{10,6},{11,7},{12,8},{13,9},{1... | collective-permute-start | bytes 196616 | tf_op jit(solution)/shard_map/ppermute | solution.py:12
  23.1 3.0 %collective-permute-start.1 = (bf16[64,512]{1,0:T(8,128)(2,1)S(1)}, bf16[64,512]{1,0:T(8,128)(2,1)S(1)}, u32[]{:S(2)}, u32[]{:S(2)}) collective-permute-start(bf16[64,512]{1,0:T(8,128)(2,1)S(1)} %get-tuple-element.11), channel_id=1, source_target_pairs={{3,0},{4,1},{5,2},{6,3},{7,4},{8,5},{9,6},{10,7},{11,8},{12,9},{13... | collective-permute-start | bytes 196616 | tf_op jit(solution)/shard_map/ppermute | solution.py:12
  26.1 2.2 %collective-permute-start.2 = (bf16[64,512]{1,0:T(8,128)(2,1)S(1)}, bf16[64,512]{1,0:T(8,128)(2,1)S(1)}, u32[]{:S(2)}, u32[]{:S(2)}) collective-permute-start(bf16[64,512]{1,0:T(8,128)(2,1)S(1)} %get-tuple-element.10), channel_id=1, source_target_pairs={{2,0},{3,1},{4,2},{5,3},{6,4},{7,5},{8,6},{9,7},{10,8},{11,9},{12,... | collective-permute-start | bytes 196616 | tf_op jit(solution)/shard_map/ppermute | solution.py:12
  28.3 2.0 %collective-permute-start.3 = (bf16[64,512]{1,0:T(8,128)(2,1)S(1)}, bf16[64,512]{1,0:T(8,128)(2,1)S(1)}, u32[]{:S(2)}, u32[]{:S(2)}) collective-permute-start(bf16[64,512]{1,0:T(8,128)(2,1)S(1)} %get-tuple-element.9), channel_id=1, source_target_pairs={{1,0},{2,1},{3,2},{4,3},{5,4},{6,5},{7,6},{8,7},{9,8},{10,9},{11,1... | collective-permute-start | bytes 196616 | tf_op jit(solution)/shard_map/ppermute | solution.py:12
  30.3 3.5 %collective-permute-start.4 = (bf16[64,512]{1,0:T(8,128)(2,1)S(1)}, bf16[64,512]{1,0:T(8,128)(2,1)S(1)}, u32[]{:S(2)}, u32[]{:S(2)}) collective-permute-start(bf16[64,512]{1,0:T(8,128)(2,1)S(1)} %get-tuple-element.8), channel_id=1, source_target_pairs={{127,0},{0,1},{1,2},{2,3},{3,4},{4,5},{5,6},{6,7},{7,8},{8,9},{9,1... | collective-permute-start | bytes 196616 | tf_op jit(solution)/shard_map/ppermute | solution.py:12
  34.6 0.0 collective-permute-done
  34.6 3.1 %collective-permute-start.5 = (bf16[64,512]{1,0:T(8,128)(2,1)S(1)}, bf16[64,512]{1,0:T(8,128)(2,1)S(1)}, u32[]{:S(2)}, u32[]{:S(2)}) collective-permute-start(bf16[64,512]{1,0:T(8,128)(2,1)S(1)} %get-tuple-element.7), channel_id=1, source_target_pairs={{126,0},{127,1},{0,2},{1,3},{2,4},{3,5},{4,6},{5,7},{6,8},{7,9},{8... | collective-permute-start | bytes 196616 | tf_op jit(solution)/shard_map/ppermute | solution.py:12
  37.7 0.0 collective-permute-done.1
  37.7 3.1 %collective-permute-start.6 = (bf16[64,512]{1,0:T(8,128)(2,1)S(1)}, bf16[64,512]{1,0:T(8,128)(2,1)S(1)}, u32[]{:S(2)}, u32[]{:S(2)}) collective-permute-start(bf16[64,512]{1,0:T(8,128)(2,1)S(1)} %get-tuple-element.6), channel_id=1, source_target_pairs={{125,0},{126,1},{127,2},{0,3},{1,4},{2,5},{3,6},{4,7},{5,8},{6,9},... | collective-permute-start | bytes 196616 | tf_op jit(solution)/shard_map/ppermute | solution.py:12
  40.8 0.0 collective-permute-done.2
  40.8 4.0 %collective-permute-start.7 = (bf16[64,512]{1,0:T(8,128)(2,1)S(1)}, bf16[64,512]{1,0:T(8,128)(2,1)S(1)}, u32[]{:S(2)}, u32[]{:S(2)}) collective-permute-start(bf16[64,512]{1,0:T(8,128)(2,1)S(1)} %get-tuple-element.5), channel_id=1, source_target_pairs={{124,0},{125,1},{126,2},{127,3},{0,4},{1,5},{2,6},{3,7},{4,8},{5,9... | collective-permute-start | bytes 196616 | tf_op jit(solution)/shard_map/ppermute | solution.py:12
  44.9 0.0 collective-permute-done.4
  45.0 0.0 collective-permute-done.5
  45.0 2.5 %collective-permute-done.6 = bf16[64,512]{1,0:T(8,128)(2,1)S(1)} collective-permute-done((bf16[64,512]{1,0:T(8,128)(2,1)S(1)}, bf16[64,512]{1,0:T(8,128)(2,1)S(1)}, u32[]{:S(2)}, u32[]{:S(2)}) %collective-permute-start.6) | collective-permute-done | bytes 65568 | tf_op jit(solution)/shard_map/ppermute | solution.py:12
  47.4 2.6 %collective-permute-done.7 = bf16[64,512]{1,0:T(8,128)(2,1)S(1)} collective-permute-done((bf16[64,512]{1,0:T(8,128)(2,1)S(1)}, bf16[64,512]{1,0:T(8,128)(2,1)S(1)}, u32[]{:S(2)}, u32[]{:S(2)}) %collective-permute-start.7) | collective-permute-done | bytes 65568 | tf_op jit(solution)/shard_map/ppermute | solution.py:12
  50.1 0.2 fusion.26
  50.3 0.0 copy-start.1
  50.3 0.7 copy-done.1
  51.0 0.3 fusion.28
  51.3 3.5 %gather_fusion = f32[1024,512]{1,0:T(8,128)S(1)} fusion(f32[128,512]{1,0:T(8,128)S(1)} %fusion.28, s32[1024]{0:T(1024)S(1)} %broadcast_clamp_fusion), kind=kCustom, calls=%fused_computation | custom fusion | bytes 4198400 | tf_op jit(solution)/shard_map/jit(_take)/gather | solution.py:60
  54.9 0.0 copy-start.7
  54.9 5.5 %convolution_convert_fusion = bf16[1024,1024]{1,0:T(8,128)(2,1)} fusion(bf16[1024,512]{1,0:T(8,128)(2,1)S(1)} %copy-done, f32[1024,512]{1,0:T(8,128)S(1)} %gather_fusion, bf16[512,512]{1,0:T(8,128)(2,1)} %param.21, bf16[1,1024,512]{2,1,0:T(8,128)(2,1)} %param.11, bf16[1,1024,512]{2,1,0:T(8,128)(2,1)} %param.12, pred[1024]{0:T(1024)(128)(4,1)S(1)} %get-tuple-element.22, ...), kind=kOutput, calls=%fused_computation.13 | convolution fusion | flops 1618477056 | bytes 7866368 | tf_op jit(solution)/shard_map/dot_general | solution.py:66
  60.4 1.6 %fusion.19 = f32[128,512]{1,0:T(8,128)S(1)} fusion(bf16[1024,1024]{1,0:T(8,128)(2,1)} %convolution_convert_fusion, s32[1024]{0:T(1024)S(1)} %bitcast.50, s32[128]{0:T(128)S(1)} %iota_add_fusion), kind=kOutput, calls=%fused_computation.25 | convolution fusion | flops 134348800 | bytes 1315328 | tf_op jit(solution)/shard_map/dot_general | solution.py:79
  62.0 0.0 copy-start.6
  62.0 2.2 %collective-permute-start.8 = (f32[16,512]{1,0:T(8,128)S(1)}, f32[16,512]{1,0:T(8,128)S(1)}, u32[]{:S(2)}, u32[]{:S(2)}) collective-permute-start(f32[16,512]{1,0:T(8,128)S(1)} %get-tuple-element.20), channel_id=1, source_target_pairs={{4,0},{5,1},{6,2},{7,3},{8,4},{9,5},{10,6},{11,7},{12,8},{13,9},{1... | collective-permute-start | bytes 98312 | tf_op jit(solution)/shard_map/ppermute | solution.py:12
  64.2 1.9 %fusion.8 = f32[512,512]{1,0:T(8,128)S(1)} fusion(s32[1024]{0:T(1024)S(1)} %bitcast.51, bf16[1024,1024]{1,0:T(8,128)(2,1)} %convolution_convert_fusion), kind=kOutput, calls=%fused_computation.12 | convolution fusion | flops 537395200 | bytes 2101248 | tf_op jit(solution)/shard_map/dot_general | solution.py:97
  66.2 0.0 copy-start.2
  66.2 5.6 %collective-permute-start.9 = (f32[16,512]{1,0:T(8,128)S(1)}, f32[16,512]{1,0:T(8,128)S(1)}, u32[]{:S(2)}, u32[]{:S(2)}) collective-permute-start(f32[16,512]{1,0:T(8,128)S(1)} %get-tuple-element.19), channel_id=1, source_target_pairs={{3,0},{4,1},{5,2},{6,3},{7,4},{8,5},{9,6},{10,7},{11,8},{12,9},{13... | collective-permute-start | bytes 98312 | tf_op jit(solution)/shard_map/ppermute | solution.py:12
  71.8 1.9 %collective-permute-start.10 = (f32[16,512]{1,0:T(8,128)S(1)}, f32[16,512]{1,0:T(8,128)S(1)}, u32[]{:S(2)}, u32[]{:S(2)}) collective-permute-start(f32[16,512]{1,0:T(8,128)S(1)} %get-tuple-element.18), channel_id=1, source_target_pairs={{2,0},{3,1},{4,2},{5,3},{6,4},{7,5},{8,6},{9,7},{10,8},{11,9},{12,... | collective-permute-start | bytes 98312 | tf_op jit(solution)/shard_map/ppermute | solution.py:12
  73.8 2.3 %collective-permute-start.11 = (f32[16,512]{1,0:T(8,128)S(1)}, f32[16,512]{1,0:T(8,128)S(1)}, u32[]{:S(2)}, u32[]{:S(2)}) collective-permute-start(f32[16,512]{1,0:T(8,128)S(1)} %get-tuple-element.17), channel_id=1, source_target_pairs={{1,0},{2,1},{3,2},{4,3},{5,4},{6,5},{7,6},{8,7},{9,8},{10,9},{11,1... | collective-permute-start | bytes 98312 | tf_op jit(solution)/shard_map/ppermute | solution.py:12
  76.1 3.3 %collective-permute-start.12 = (f32[16,512]{1,0:T(8,128)S(1)}, f32[16,512]{1,0:T(8,128)S(1)}, u32[]{:S(2)}, u32[]{:S(2)}) collective-permute-start(f32[16,512]{1,0:T(8,128)S(1)} %get-tuple-element.16), channel_id=1, source_target_pairs={{127,0},{0,1},{1,2},{2,3},{3,4},{4,5},{5,6},{6,7},{7,8},{8,9},{9,1... | collective-permute-start | bytes 98312 | tf_op jit(solution)/shard_map/ppermute | solution.py:12
  79.3 0.0 collective-permute-done.8
  79.4 3.4 %collective-permute-start.13 = (f32[16,512]{1,0:T(8,128)S(1)}, f32[16,512]{1,0:T(8,128)S(1)}, u32[]{:S(2)}, u32[]{:S(2)}) collective-permute-start(f32[16,512]{1,0:T(8,128)S(1)} %get-tuple-element.15), channel_id=1, source_target_pairs={{126,0},{127,1},{0,2},{1,3},{2,4},{3,5},{4,6},{5,7},{6,8},{7,9},{8... | collective-permute-start | bytes 98312 | tf_op jit(solution)/shard_map/ppermute | solution.py:12
  82.7 2.5 %collective-permute-start.14 = (f32[16,512]{1,0:T(8,128)S(1)}, f32[16,512]{1,0:T(8,128)S(1)}, u32[]{:S(2)}, u32[]{:S(2)}) collective-permute-start(f32[16,512]{1,0:T(8,128)S(1)} %get-tuple-element.14), channel_id=1, source_target_pairs={{125,0},{126,1},{127,2},{0,3},{1,4},{2,5},{3,6},{4,7},{5,8},{6,9},... | collective-permute-start | bytes 98312 | tf_op jit(solution)/shard_map/ppermute | solution.py:12
  85.3 0.0 collective-permute-done.10
  85.3 5.4 %collective-permute-start.15 = (f32[16,512]{1,0:T(8,128)S(1)}, f32[16,512]{1,0:T(8,128)S(1)}, u32[]{:S(2)}, u32[]{:S(2)}) collective-permute-start(f32[16,512]{1,0:T(8,128)S(1)} %get-tuple-element.13), channel_id=1, source_target_pairs={{124,0},{125,1},{126,2},{127,3},{0,4},{1,5},{2,6},{3,7},{4,8},{5,9... | collective-permute-start | bytes 98312 | tf_op jit(solution)/shard_map/ppermute | solution.py:12
  90.7 0.0 collective-permute-done.11
  90.7 0.0 collective-permute-done.12
  90.8 0.5 collective-permute-done.14
  91.3 2.9 %collective-permute-done.15 = f32[16,512]{1,0:T(8,128)S(1)} collective-permute-done((f32[16,512]{1,0:T(8,128)S(1)}, f32[16,512]{1,0:T(8,128)S(1)}, u32[]{:S(2)}, u32[]{:S(2)}) %collective-permute-start.15) | collective-permute-done | bytes 32800 | tf_op jit(solution)/shard_map/ppermute | solution.py:12
  94.2 1.6 %convolution_add_fusion = f32[512,512]{1,0:T(8,128)} fusion(f32[512,512]{1,0:T(8,128)S(1)} %fusion.8, f32[128,512]{1,0:T(8,128)S(1)} %constant_dynamic-update-slice_fusion.8, s32[128]{0:T(128)S(1)} %bitcast.49), kind=kOutput, calls=%fused_computation.14 | convolution fusion | flops 402980864 | bytes 2359808 | tf_op jit(solution)/shard_map/dot_general | solution.py:91
  95.8 0.0 reduce-scatter.2.cloned.1.call-update
  95.8 1.5 %convolution_add_fusion.1 = f32[128,512]{1,0:T(8,128)S(1)} fusion(f32[128,512]{1,0:T(8,128)S(1)} %copy-done.2, bf16[1024,1024]{1,0:T(8,128)(2,1)} %convolution_convert_fusion, s32[1024]{0:T(1024)S(1)} %bitcast.47), kind=kOutput, calls=%fused_computation.15 | convolution fusion | flops 134414336 | bytes 1576960 | tf_op jit(solution)/shard_map/dot_general | solution.py:72
  97.4 22.3 %reduce-scatter.2.cloned.1.call-done = f32[128,512]{1,0:T(8,128)} async-done(((f32[512,512]{1,0:T(8,128)}), f32[128,512]{1,0:T(8,128)}) %reduce-scatter.2.cloned.1.call-update) | async-done | bytes 262160 | tf_op jit(solution)/shard_map/reduce_scatter | solution.py:98
  119.7 1.7 %add_bitcast_fusion = f32[1,128,512]{2,1,0:T(8,128)} fusion(f32[128,512]{1,0:T(8,128)S(1)} %convolution_add_fusion.1, f32[128,512]{1,0:T(8,128)} %reduce-scatter.2.cloned.1.call-done), kind=kLoop, calls=%fused_computation.31 | loop fusion | flops 65536 | bytes 786432 | tf_op jit(solution)/shard_map/broadcast_in_dim | solution.py:99
  (36 shorter events, 0.2 us)
Async XLA Ops:
  6.5 48.3 %copy-start = (bf16[1024,512]{1,0:T(8,128)(2,1)S(1)}, bf16[1024,512]{1,0:T(8,128)(2,1)}, u32[]{:S(2)}) copy-start(bf16[1024,512]{1,0:T(8,128)(2,1)} %param.20) | copy-start | bytes 3145732
  6.5 27.3 %copy-start.4 = (s32[1,1024]{1,0:T(1,128)S(1)}, s32[1,1024]{1,0:T(1,128)}, u32[]{:S(2)}) copy-start(s32[1,1024]{1,0:T(1,128)} %param.13) | copy-start | bytes 12292
  6.5 43.5 %copy-start.5 = (s32[1,512]{1,0:T(1,128)S(1)}, s32[1,512]{1,0:T(1,128)}, u32[]{:S(2)}) copy-start(s32[1,512]{1,0:T(1,128)} %param.19) | copy-start | bytes 6148
  6.5 44.5 %copy-start.3 = (bf16[512,512]{1,0:T(8,128)(2,1)S(1)}, bf16[512,512]{1,0:T(8,128)(2,1)}, u32[]{:S(2)}) copy-start(bf16[512,512]{1,0:T(8,128)(2,1)} %param.21) | copy-start | bytes 1572868
  6.5 113.1 %reduce-scatter.2.cloned.1.call-start = ((), (), s32[]{:S(2)}) async-start(), calls=%async_computation.1 | async-start | bytes 1310720 | tf_op jit(solution)/shard_map/reduce_scatter | solution.py:98
  8.7 25.9 %collective-permute-start = (bf16[64,512]{1,0:T(8,128)(2,1)S(1)}, bf16[64,512]{1,0:T(8,128)(2,1)S(1)}, u32[]{:S(2)}, u32[]{:S(2)}) collective-permute-start(bf16[64,512]{1,0:T(8,128)(2,1)S(1)} %get-tuple-element.12), channel_id=1, source_target_pairs={{4,0},{5,1},{6,2},{7,3},{8,4},{9,5},{10,6},{11,7},{12,8},{13,9},{1... | collective-permute-start | bytes 196616 | tf_op jit(solution)/shard_map/ppermute | solution.py:12
  23.1 14.6 %collective-permute-start.1 = (bf16[64,512]{1,0:T(8,128)(2,1)S(1)}, bf16[64,512]{1,0:T(8,128)(2,1)S(1)}, u32[]{:S(2)}, u32[]{:S(2)}) collective-permute-start(bf16[64,512]{1,0:T(8,128)(2,1)S(1)} %get-tuple-element.11), channel_id=1, source_target_pairs={{3,0},{4,1},{5,2},{6,3},{7,4},{8,5},{9,6},{10,7},{11,8},{12,9},{13... | collective-permute-start | bytes 196616 | tf_op jit(solution)/shard_map/ppermute | solution.py:12
  26.1 14.8 %collective-permute-start.2 = (bf16[64,512]{1,0:T(8,128)(2,1)S(1)}, bf16[64,512]{1,0:T(8,128)(2,1)S(1)}, u32[]{:S(2)}, u32[]{:S(2)}) collective-permute-start(bf16[64,512]{1,0:T(8,128)(2,1)S(1)} %get-tuple-element.10), channel_id=1, source_target_pairs={{2,0},{3,1},{4,2},{5,3},{6,4},{7,5},{8,6},{9,7},{10,8},{11,9},{12,... | collective-permute-start | bytes 196616 | tf_op jit(solution)/shard_map/ppermute | solution.py:12
  28.3 16.6 %collective-permute-start.3 = (bf16[64,512]{1,0:T(8,128)(2,1)S(1)}, bf16[64,512]{1,0:T(8,128)(2,1)S(1)}, u32[]{:S(2)}, u32[]{:S(2)}) collective-permute-start(bf16[64,512]{1,0:T(8,128)(2,1)S(1)} %get-tuple-element.9), channel_id=1, source_target_pairs={{1,0},{2,1},{3,2},{4,3},{5,4},{6,5},{7,6},{8,7},{9,8},{10,9},{11,1... | collective-permute-start | bytes 196616 | tf_op jit(solution)/shard_map/ppermute | solution.py:12
  30.3 14.6 %collective-permute-start.4 = (bf16[64,512]{1,0:T(8,128)(2,1)S(1)}, bf16[64,512]{1,0:T(8,128)(2,1)S(1)}, u32[]{:S(2)}, u32[]{:S(2)}) collective-permute-start(bf16[64,512]{1,0:T(8,128)(2,1)S(1)} %get-tuple-element.8), channel_id=1, source_target_pairs={{127,0},{0,1},{1,2},{2,3},{3,4},{4,5},{5,6},{6,7},{7,8},{8,9},{9,1... | collective-permute-start | bytes 196616 | tf_op jit(solution)/shard_map/ppermute | solution.py:12
  34.6 10.4 %collective-permute-start.5 = (bf16[64,512]{1,0:T(8,128)(2,1)S(1)}, bf16[64,512]{1,0:T(8,128)(2,1)S(1)}, u32[]{:S(2)}, u32[]{:S(2)}) collective-permute-start(bf16[64,512]{1,0:T(8,128)(2,1)S(1)} %get-tuple-element.7), channel_id=1, source_target_pairs={{126,0},{127,1},{0,2},{1,3},{2,4},{3,5},{4,6},{5,7},{6,8},{7,9},{8... | collective-permute-start | bytes 196616 | tf_op jit(solution)/shard_map/ppermute | solution.py:12
  37.7 9.7 %collective-permute-start.6 = (bf16[64,512]{1,0:T(8,128)(2,1)S(1)}, bf16[64,512]{1,0:T(8,128)(2,1)S(1)}, u32[]{:S(2)}, u32[]{:S(2)}) collective-permute-start(bf16[64,512]{1,0:T(8,128)(2,1)S(1)} %get-tuple-element.6), channel_id=1, source_target_pairs={{125,0},{126,1},{127,2},{0,3},{1,4},{2,5},{3,6},{4,7},{5,8},{6,9},... | collective-permute-start | bytes 196616 | tf_op jit(solution)/shard_map/ppermute | solution.py:12
  40.8 9.2 %collective-permute-start.7 = (bf16[64,512]{1,0:T(8,128)(2,1)S(1)}, bf16[64,512]{1,0:T(8,128)(2,1)S(1)}, u32[]{:S(2)}, u32[]{:S(2)}) collective-permute-start(bf16[64,512]{1,0:T(8,128)(2,1)S(1)} %get-tuple-element.5), channel_id=1, source_target_pairs={{124,0},{125,1},{126,2},{127,3},{0,4},{1,5},{2,6},{3,7},{4,8},{5,9... | collective-permute-start | bytes 196616 | tf_op jit(solution)/shard_map/ppermute | solution.py:12
  50.3 0.7 copy-start.1
  54.9 5.5 %copy-start.7 = (s32[1,1024]{1,0:T(1,128)S(1)}, s32[1,1024]{1,0:T(1,128)}, u32[]{:S(2)}) copy-start(s32[1,1024]{1,0:T(1,128)} %param.14) | copy-start | bytes 12292
  62.0 32.2 %copy-start.6 = (s32[1,1,128]{2,1,0:T(1,128)S(1)}, s32[1,1,128]{2,1,0:T(1,128)}, u32[]{:S(2)}) copy-start(s32[1,1,128]{2,1,0:T(1,128)} %param.16) | copy-start | bytes 1540
  62.0 17.4 %collective-permute-start.8 = (f32[16,512]{1,0:T(8,128)S(1)}, f32[16,512]{1,0:T(8,128)S(1)}, u32[]{:S(2)}, u32[]{:S(2)}) collective-permute-start(f32[16,512]{1,0:T(8,128)S(1)} %get-tuple-element.20), channel_id=1, source_target_pairs={{4,0},{5,1},{6,2},{7,3},{8,4},{9,5},{10,6},{11,7},{12,8},{13,9},{1... | collective-permute-start | bytes 98312 | tf_op jit(solution)/shard_map/ppermute | solution.py:12
  66.2 29.6 %copy-start.2 = (f32[128,512]{1,0:T(8,128)S(1)}, f32[128,512]{1,0:T(8,128)}, u32[]{:S(2)}) copy-start(f32[128,512]{1,0:T(8,128)} %copy-done.1) | copy-start | bytes 786436
  66.2 16.5 %collective-permute-start.9 = (f32[16,512]{1,0:T(8,128)S(1)}, f32[16,512]{1,0:T(8,128)S(1)}, u32[]{:S(2)}, u32[]{:S(2)}) collective-permute-start(f32[16,512]{1,0:T(8,128)S(1)} %get-tuple-element.19), channel_id=1, source_target_pairs={{3,0},{4,1},{5,2},{6,3},{7,4},{8,5},{9,6},{10,7},{11,8},{12,9},{13... | collective-permute-start | bytes 98312 | tf_op jit(solution)/shard_map/ppermute | solution.py:12
  71.8 13.4 %collective-permute-start.10 = (f32[16,512]{1,0:T(8,128)S(1)}, f32[16,512]{1,0:T(8,128)S(1)}, u32[]{:S(2)}, u32[]{:S(2)}) collective-permute-start(f32[16,512]{1,0:T(8,128)S(1)} %get-tuple-element.18), channel_id=1, source_target_pairs={{2,0},{3,1},{4,2},{5,3},{6,4},{7,5},{8,6},{9,7},{10,8},{11,9},{12,... | collective-permute-start | bytes 98312 | tf_op jit(solution)/shard_map/ppermute | solution.py:12
  73.8 16.9 %collective-permute-start.11 = (f32[16,512]{1,0:T(8,128)S(1)}, f32[16,512]{1,0:T(8,128)S(1)}, u32[]{:S(2)}, u32[]{:S(2)}) collective-permute-start(f32[16,512]{1,0:T(8,128)S(1)} %get-tuple-element.17), channel_id=1, source_target_pairs={{1,0},{2,1},{3,2},{4,3},{5,4},{6,5},{7,6},{8,7},{9,8},{10,9},{11,1... | collective-permute-start | bytes 98312 | tf_op jit(solution)/shard_map/ppermute | solution.py:12
  76.1 14.6 %collective-permute-start.12 = (f32[16,512]{1,0:T(8,128)S(1)}, f32[16,512]{1,0:T(8,128)S(1)}, u32[]{:S(2)}, u32[]{:S(2)}) collective-permute-start(f32[16,512]{1,0:T(8,128)S(1)} %get-tuple-element.16), channel_id=1, source_target_pairs={{127,0},{0,1},{1,2},{2,3},{3,4},{4,5},{5,6},{6,7},{7,8},{8,9},{9,1... | collective-permute-start | bytes 98312 | tf_op jit(solution)/shard_map/ppermute | solution.py:12
  79.4 11.4 %collective-permute-start.13 = (f32[16,512]{1,0:T(8,128)S(1)}, f32[16,512]{1,0:T(8,128)S(1)}, u32[]{:S(2)}, u32[]{:S(2)}) collective-permute-start(f32[16,512]{1,0:T(8,128)S(1)} %get-tuple-element.15), channel_id=1, source_target_pairs={{126,0},{127,1},{0,2},{1,3},{2,4},{3,5},{4,6},{5,7},{6,8},{7,9},{8... | collective-permute-start | bytes 98312 | tf_op jit(solution)/shard_map/ppermute | solution.py:12
  82.7 8.6 %collective-permute-start.14 = (f32[16,512]{1,0:T(8,128)S(1)}, f32[16,512]{1,0:T(8,128)S(1)}, u32[]{:S(2)}, u32[]{:S(2)}) collective-permute-start(f32[16,512]{1,0:T(8,128)S(1)} %get-tuple-element.14), channel_id=1, source_target_pairs={{125,0},{126,1},{127,2},{0,3},{1,4},{2,5},{3,6},{4,7},{5,8},{6,9},... | collective-permute-start | bytes 98312 | tf_op jit(solution)/shard_map/ppermute | solution.py:12
  85.3 8.9 %collective-permute-start.15 = (f32[16,512]{1,0:T(8,128)S(1)}, f32[16,512]{1,0:T(8,128)S(1)}, u32[]{:S(2)}, u32[]{:S(2)}) collective-permute-start(f32[16,512]{1,0:T(8,128)S(1)} %get-tuple-element.13), channel_id=1, source_target_pairs={{124,0},{125,1},{126,2},{127,3},{0,4},{1,5},{2,6},{3,7},{4,8},{5,9... | collective-permute-start | bytes 98312 | tf_op jit(solution)/shard_map/ppermute | solution.py:12
Sparse Core Ops, SparseCore 0:
  95.9 23.7 reduce-scatter.1
where the time goes:
time: 129 us; the launch traced here: 128 us
  starting transfers between devices  62 us (48%)
  waiting for transfers between devices  30.9 us (24%)
  between operations  14.5 us (11%)
  matrix products  12.7 us (10%)
  local copies, waits for them, and re-layouts  4.39 us (3%)
  other arithmetic  3.72 us (3%)
    ppermute x16, starting transfers between devices, from_behind(): return lax.ppermute(block, axis, route)  62 us
    reduce_scatter x1, waiting for transfers between devices, per_device(): lax.psum_scatter(send_total + landed, 'sec', scatter_dimension=0, tiled=T...  22.3 us
    ppermute x16, waiting for transfers between devices, from_behind(): return lax.ppermute(block, axis, route)  8.54 us
    dot_general x1, matrix products, per_device(): lax.dot_general(delta_pre, w_node, contract_last, preferred_element_type=...  5.49 us
    gather x1, local copies, waits for them, and re-layouts, per_device(): delta_act = jnp.take(node_proj, recv_local[0], axis=0) + edge_proj  3.51 us
  transfers between devices with their start and end apart: 17, of which 5 were waited for; matrix products, arithmetic and copies ran while one was open for 3% of the time, Pallas kernels for 0%

commit v1 on v0

v1 whole, which is shorter than its diff:
```python
import functools

import jax
import jax.numpy as jnp
from jax import lax
from jax.experimental import pallas as pl
from jax.experimental.pallas import tpu as pltpu
from jax.sharding import PartitionSpec as P

MESH = pl.DeviceIdType.MESH
QUART = 128
GROUP = 4
NT = (((1,), (1,)), ((), ()))
F32 = jnp.float32
BF16 = jnp.bfloat16


def offset_value(number, neighbours):
    half = neighbours // 2
    return number - half + 1 if number >= half else number - half


def iota(shape, dim):
    return lax.broadcasted_iota(jnp.int32, shape, dim)


def hot(mask):
    return jnp.where(mask, F32(1.0), F32(0.0)).astype(BF16)


def dot(a, b):
    return jnp.dot(a, b, preferred_element_type=F32)


def dot_nt(a, b):
    return lax.dot_general(a, b, NT, preferred_element_type=F32)


def kernel(
    sec_count,
    tile_count,
    neighbours,
    pre_hbm,
    cot_hbm,
    recv_hbm,
    slot_hbm,
    ecnt_hbm,
    hmap_hbm,
    dec_hbm,
    dcnt_hbm,
    dnode_hbm,
    wnode_hbm,
    wout_hbm,
    out_ref,
    pre,
    cot,
    recv,
    slot,
    ecnt,
    hmap,
    dec,
    dcnt,
    dnode,
    wnode,
    wout,
    edge_proj,
    slope,
    delta,
    hot_edge,
    hot_sums,
    hot_dec,
    hot_land,
    node_split,
    node_cot,
    base,
    sums,
    dec_out,
    dec_in,
    halo_out,
    halo_in,
    ring_out,
    ring_in,
    load_sem,
    dec_send,
    dec_recv,
    halo_send,
    halo_recv,
    ring_send,
    ring_recv,
):
    edges, latent = cot.shape
    rows = dec.shape[0]
    groups = dec_in.shape[0]
    block = groups // neighbours
    capacity = rows // neighbours
    halo = halo_in.shape[0]
    half = latent // 2
    local_rows = sec_count * QUART
    sec = lax.axis_index("sec")
    tile = lax.axis_index("tile")
    right = lax.rem(sec + 1, sec_count)
    left = lax.rem(sec + sec_count - 1, sec_count)
    peers = [
        lax.rem(tile + offset_value(o, neighbours) + tile_count, tile_count)
        for o in range(neighbours)
    ]

    sources = [
        (dec_hbm.at[0], dec),
        (dcnt_hbm, dcnt),
        (cot_hbm.at[0], cot),
        (wout_hbm, wout),
        (pre_hbm.at[0], pre),
        (recv_hbm, recv),
        (slot_hbm, slot),
        (ecnt_hbm, ecnt),
        (dnode_hbm, dnode),
        (hmap_hbm.at[0], hmap),
        (wnode_hbm, wnode),
    ]
    loads = [
        pltpu.make_async_copy(src, dst, load_sem.at[i]) for i, (src, dst) in enumerate(sources)
    ]
    for load in loads:
        load.start()

    barrier = pltpu.get_barrier_semaphore()
    for peer in peers:
        pl.semaphore_signal(barrier, inc=1, device_id=(sec, peer), device_id_type=MESH)
    for peer in (left, right):
        pl.semaphore_signal(barrier, inc=1, device_id=(peer, tile), device_id_type=MESH)

    loads[1].wait()
    loads[0].wait()
    lane = iota((1, rows), 1)
    count = jnp.zeros((1, rows), jnp.int32)
    for o in range(neighbours):
        count = jnp.where(lane // capacity == o, dcnt[0:1, o : o + 1], count)
    live_lane = jnp.where(lane % capacity < count, lane // GROUP, -1)
    pick = hot(iota((groups, rows), 0) == live_lane)
    dec_out[...] = dot(pick, dec[...]).astype(BF16)

    pl.semaphore_wait(barrier, neighbours + 2)

    def tile_copies(src, dst, send, recv_sems):
        return [
            pltpu.make_async_remote_copy(
                src_ref=src.at[pl.ds(o * block, block)],
                dst_ref=dst.at[pl.ds(o * block, block)],
                send_sem=send.at[o],
                recv_sem=recv_sems.at[o],
                device_id=(sec, peers[o]),
                device_id_type=MESH,
            )
            for o in range(neighbours)
        ]

    dec_copies = tile_copies(dec_out, dec_in, dec_send, dec_recv)
    for copy in dec_copies:
        copy.start()

    for load in loads[2:10]:
        load.wait()
    step = 256

    def edge_block(i, carry):
        at = pl.ds(i * step, step)
        edge_proj[at, :] = dot_nt(cot[at, :], wout[...])
        v = pre[at, :].astype(F32)
        s = jax.nn.sigmoid(v)
        slope[at, :] = s * (1.0 + v * (1.0 - s))
        return carry

    lax.fori_loop(0, edges // step, edge_block, 0)

    node_row = iota((QUART, edges), 0)
    receivers = recv[...]
    edge_hot = jnp.where(node_row == receivers, F32(1.0), F32(0.0)).T.astype(BF16)
    hot_edge[:, :QUART] = edge_hot
    hot_edge[:, QUART:] = edge_hot
    live = iota((1, edges), 1) < ecnt[...]
    live_slot = jnp.where(live, slot[...], -1)
    live_recv = jnp.where(live, receivers, -1)
    hot_sums[0:QUART, :] = hot(node_row == live_slot - local_rows)
    order = (2, 1, 3, 0)
    for i, k in enumerate(order):
        quarter = lax.rem(sec + k, sec_count)
        hot_sums[(i + 1) * QUART : (i + 2) * QUART, :] = hot(
            node_row == live_slot - quarter * QUART
        )
        hot_land[i * QUART : (i + 1) * QUART, :] = hot(
            iota((QUART, halo), 0) == hmap[...] - quarter * QUART
        )
    hot_sums[5 * QUART : 6 * QUART, :] = hot(node_row == live_recv)
    first_of_group = jnp.where(lane % GROUP == 0, dnode[...], -1)
    named = hot(iota((QUART, rows), 0) == first_of_group)
    group_of = hot(iota((groups, rows), 0) == lane // GROUP)
    hot_dec[...] = dot_nt(named, group_of).astype(BF16)

    for copy in dec_copies:
        copy.wait_recv()
    cot_sum = dot(hot_dec[...], dec_in[...])
    node_cot[...] = cot_sum
    node_proj = dot_nt(cot_sum.astype(BF16), wout[...])
    high = node_proj.astype(BF16)
    node_split[:QUART, :] = high
    node_split[QUART:, :] = (node_proj - high.astype(F32)).astype(BF16)

    def delta_block(i, carry):
        at = pl.ds(i * step, step)
        act = edge_proj[at, :] + dot(hot_edge[at, :], node_split[...])
        delta[at, :] = (act * slope[at, :]).astype(BF16)
        return carry

    lax.fori_loop(0, edges // step, delta_block, 0)

    halo_out[...] = dot(hot_sums[0:QUART, :], delta[...]).astype(BF16)
    halo_copies = tile_copies(halo_out, halo_in, halo_send, halo_recv)
    for copy in halo_copies:
        copy.start()

    def sum_block(i, carry):
        at = pl.ds(i * QUART, QUART)
        sums[at, :] = dot(hot_sums[pl.ds((i + 1) * QUART, QUART), :], delta[...])
        return carry

    lax.fori_loop(0, 5, sum_block, 0)

    loads[10].wait()
    for copy in halo_copies:
        copy.wait_recv()

    def ring_copy(i, peer):
        return pltpu.make_async_remote_copy(
            src_ref=ring_out.at[i],
            dst_ref=ring_in.at[i],
            send_sem=ring_send.at[i],
            recv_sem=ring_recv.at[i],
            device_id=(peer, tile),
            device_id_type=MESH,
        )

    ring = [ring_copy(i, right if i % 2 == 0 else left) for i in range(6)]

    def with_landed(i):
        at = slice(i * QUART, (i + 1) * QUART)
        return sums[at, :] + dot(hot_land[at, :], halo_in[...])

    far = with_landed(0)
    ring_out[0] = far[:, :half].astype(BF16)
    ring_out[1] = far[:, half:].astype(BF16)
    ring[0].start()
    ring[1].start()
    ahead = with_landed(1)
    ring_out[2] = ahead[:, half:].astype(BF16)
    ring[2].start()
    behind = with_landed(2)
    ring_out[3] = behind[:, :half].astype(BF16)
    ring[3].start()
    ring[0].wait_recv()
    ring_out[4] = (ahead[:, :half] + ring_in[0].astype(F32)).astype(BF16)
    ring[4].start()
    ring[1].wait_recv()
    ring_out[5] = (behind[:, half:] + ring_in[1].astype(F32)).astype(BF16)
    ring[5].start()

    sums[3 * QUART : 4 * QUART, :] = with_landed(3)
    received = sums[4 * QUART : 5 * QUART, :].astype(BF16)
    base[...] = node_cot[...] + dot_nt(received, wnode[latent:, :])
    for i in (2, 3, 4, 5):
        ring[i].wait_recv()
    own = sums[3 * QUART : 4 * QUART, :]
    own_a = own[:, :half] + ring_in[3].astype(F32) + ring_in[4].astype(F32)
    own_b = own[:, half:] + ring_in[2].astype(F32) + ring_in[5].astype(F32)
    out_ref[0] = (
        base[...]
        + dot_nt(own_a.astype(BF16), wnode[:latent, :half])
        + dot_nt(own_b.astype(BF16), wnode[:latent, half:])
    )
    for copy in dec_copies + halo_copies + ring:
        copy.wait_send()


def per_device(
    pre_act,
    edge_cot,
    recv_local,
    send_slot,
    edge_count,
    halo_map,
    dec_rows,
    dec_count,
    dec_node,
    w_node,
    w_out,
):
    sec_count = lax.axis_size("sec")
    tile_count = lax.axis_size("tile")
    edges, latent = pre_act.shape[1:]
    rows = dec_rows.shape[1]
    neighbours = dec_count.shape[1]
    groups = rows // GROUP
    halo = halo_map.shape[2]
    half = latent // 2
    operands = (
        pre_act,
        edge_cot,
        recv_local,
        send_slot,
        edge_count,
        halo_map,
        dec_rows,
        dec_count,
        dec_node,
        w_node,
        w_out,
    )
    vmem = pltpu.VMEM
    return pl.pallas_call(
        functools.partial(kernel, sec_count, tile_count, neighbours),
        out_shape=jax.ShapeDtypeStruct((1, QUART, latent), F32),
        in_specs=[pl.BlockSpec(memory_space=pl.ANY)] * len(operands),
        out_specs=pl.BlockSpec(memory_space=pltpu.VMEM),
        scratch_shapes=[
            vmem((edges, latent), BF16),
            vmem((edges, latent), BF16),
            vmem((1, edges), jnp.int32),
            vmem((1, edges), jnp.int32),
            vmem((1, 1), jnp.int32),
            vmem((1, halo), jnp.int32),
            vmem((rows, latent), BF16),
            vmem((1, neighbours), jnp.int32),
            vmem((1, rows), jnp.int32),
            vmem(w_node.shape, BF16),
            vmem(w_out.shape, BF16),
            vmem((edges, latent), F32),
            vmem((edges, latent), F32),
            vmem((edges, latent), BF16),
            vmem((edges, 2 * QUART), BF16),
            vmem((6 * QUART, edges), BF16),
            vmem((QUART, groups), BF16),
            vmem((sec_count * QUART, halo), BF16),
            vmem((2 * QUART, latent), BF16),
            vmem((QUART, latent), F32),
            vmem((QUART, latent), F32),
            vmem((5 * QUART, latent), F32),
            vmem((groups, latent), BF16),
            vmem((groups, latent), BF16),
            vmem((halo, latent), BF16),
            vmem((halo, latent), BF16),
            vmem((6, QUART, half), BF16),
            vmem((6, QUART, half), BF16),
            pltpu.SemaphoreType.DMA((len(operands),)),
            pltpu.SemaphoreType.DMA((neighbours,)),
            pltpu.SemaphoreType.DMA((neighbours,)),
            pltpu.SemaphoreType.DMA((neighbours,)),
            pltpu.SemaphoreType.DMA((neighbours,)),
            pltpu.SemaphoreType.DMA((6,)),
            pltpu.SemaphoreType.DMA((6,)),
        ],
        compiler_params=pltpu.CompilerParams(
            collective_id=0, has_side_effects=True, vmem_limit_bytes=60 * 1024 * 1024
        ),
        cost_estimate=pl.CostEstimate(
            flops=2 * 1000 * 1000 * 1000, bytes_accessed=4 * 1024 * 1024, transcendentals=0
        ),
    )(*operands)


def solution(mesh):
    return jax.shard_map(
        per_device,
        mesh=mesh,
        in_specs=(
            P("sec", "tile", None),
            P("sec", "tile", None),
            P("sec", "tile"),
            P("sec", "tile"),
            P("sec", "tile"),
            P("sec", "tile", None),
            P("sec", "tile", None),
            P("sec", "tile"),
            P("sec", "tile"),
            P(),
            P(),
        ),
        out_specs=P("sec", "tile", None),
        check_vma=False,
    )
```

time: 129 us -> 37.4 us (0.29)
  starting transfers between devices: 62 us -> 0 us
  Pallas kernels: 0 us -> 34.3 us
  waiting for transfers between devices: 30.9 us -> 0 us
  between operations: 14.5 us -> 0.66 us
  matrix products: 12.7 us -> 0 us
  other arithmetic: 3.72 us -> 0 us
  local copies, waits for them, and re-layouts: 4.39 us -> 1.67 us
    ppermute x16 -> x0, starting transfers between devices: 62 us -> none  [from_behind(): return lax.ppermute(block, axis, route)]
    pallas_call x0 -> x1, Pallas kernels: none -> 34.3 us  [per_device(): pl.pallas_call(functools.partial(kernel, sec_count, tile_count, neighbour...]
    reduce_scatter x1 -> x0, waiting for transfers between devices: 22.3 us -> none  [per_device(): lax.psum_scatter(send_total + landed, 'sec', scatter_dimension=0, tiled=T...]
    dot_general x7 -> x0, matrix products: 12.7 us -> none  [the longest x1 5.49 us: per_device(): lax.dot_general(delta_pre, w_node, contract_last, preferred_element_type=...]
    ppermute x16 -> x0, waiting for transfers between devices: 8.54 us -> none  [from_behind(): return lax.ppermute(block, axis, route)]
    gather x1 -> x0, local copies, waits for them, and re-layouts: 3.51 us -> none  [per_device(): delta_act = jnp.take(node_proj, recv_local[0], axis=0) + edge_proj]
    broadcast_in_dim x1 -> x0, other arithmetic: 1.69 us -> none  [per_device(): return (node_cot + recv_total + own_quarter)[None]]
  transfers between devices with their start and end apart: 17 -> 0, of which waited for: 5 -> 0; matrix products, arithmetic and copies ran while one was open for 3% -> 0% of each run, Pallas kernels for 0% -> 0%
where the time goes in v1:
time: 37.4 us; the launch traced here: 36.6 us
  Pallas kernels  34.3 us (92%)
  local copies, waits for them, and re-layouts  1.67 us (4%)
  between operations  0.66 us (2%)
    pallas_call x1, Pallas kernels, per_device(): pl.pallas_call(functools.partial(kernel, sec_count, tile_count, neighbour...  34.3 us
    unnamed x1, local copies, waits for them, and re-layouts  1.67 us

profile of v1, /device:TPU:1, one launch (start us, length us, event | category | flops | bytes accessed | tf_op | source)
XLA Modules:
  0.0 36.6 jit_solution(11781870967810812664)
XLA Ops:
  0.7 34.3 %shard_map.109 = f32[1,128,512]{2,1,0:T(8,128)} custom-call(bf16[1,1024,512]{2,1,0:T(8,128)(2,1)} %pre_hbm.1, bf16[1,1024,512]{2,1,0:T(8,128)(2,1)} %cot_hbm.1, s32[1,1024]{1,0:T(1,128)} %recv_hbm.1, s32[1,1024]{1,0:T(1,128)} %slot_hbm.1, s32[1,1]{1,0:T(1,128)S(6)} %copy.13.ecnt_hbm, s32[1,1,128]{2,1,0:T(1,128)} %hmap_hbm.1, bf16[1,512,512]{2,1,0:T(8,128)(2,1)} %dec_hbm.1, ...), custom_call_target="tpu_custom_call" | custom-call | flops 2000000000 | bytes 4194304 | tf_op jit(solution)/shard_map/pallas_call | solution.py:319
  35.0 1.7 %copy.14 = f32[1,128,512]{2,1,0:T(8,128)} copy(f32[1,128,512]{2,1,0:T(8,128)} %shard_map.109) | data formatting | bytes 524288

commit v2 on v1

v2 whole, which is shorter than its diff:
```python
import functools

import jax
import jax.numpy as jnp
from jax import lax
from jax.experimental import pallas as pl
from jax.experimental.pallas import tpu as pltpu
from jax.sharding import PartitionSpec as P

MESH = pl.DeviceIdType.MESH
QUART = 128
GROUP = 4
NT = (((1,), (1,)), ((), ()))
F32 = jnp.float32
BF16 = jnp.bfloat16


def offset_value(number, neighbours):
    half = neighbours // 2
    return number - half + 1 if number >= half else number - half


def iota(shape, dim):
    return lax.broadcasted_iota(jnp.int32, shape, dim)


def hot(mask):
    return jnp.where(mask, F32(1.0), F32(0.0)).astype(BF16)


def dot(a, b):
    return jnp.dot(a, b, preferred_element_type=F32)


def dot_nt(a, b):
    return lax.dot_general(a, b, NT, preferred_element_type=F32)


def split_bf16(x):
    high = x.astype(BF16)
    return high, (x - high.astype(F32)).astype(BF16)


def kernel(
    sec_count,
    tile_count,
    neighbours,
    pre_hbm,
    cot_hbm,
    recv_hbm,
    slot_hbm,
    ecnt_smem,
    hmap_hbm,
    dec_hbm,
    dcnt_hbm,
    dnode_hbm,
    wnode_hbm,
    wout_hbm,
    out_ref,
    pre,
    cot,
    recv,
    slot,
    hmaps,
    dec,
    dcnt,
    dnode,
    wnode,
    wout,
    edge_proj,
    slope,
    delta,
    hot_edge,
    hot_sums,
    hot_dec,
    hot_land,
    node_split,
    node_cot,
    base,
    sums,
    dec_out,
    dec_in,
    halo_out,
    halo_in,
    local_out,
    local_in,
    landed_out,
    landed_in,
    load_sem,
    map_send,
    map_recv,
    dec_sem,
    halo_sem,
    local_send,
    local_recv,
    landed_send,
    landed_recv,
):
    edges, latent = cot.shape
    rows = dec.shape[0]
    groups = dec_in.shape[0]
    block = groups // neighbours
    capacity = rows // neighbours
    width = latent // sec_count
    local_rows = sec_count * QUART
    sec = lax.axis_index("sec")
    tile = lax.axis_index("tile")
    others = [lax.rem(sec + k, sec_count) for k in range(sec_count)]
    peers = [
        lax.rem(tile + offset_value(o, neighbours) + tile_count, tile_count)
        for o in range(neighbours)
    ]
    far_first = sorted(range(neighbours), key=lambda o: -abs(offset_value(o, neighbours)))

    def load(i, src, dst):
        return pltpu.make_async_copy(src, dst, load_sem.at[i])

    first_loads = [load(0, dcnt_hbm, dcnt), load(1, dec_hbm.at[0], dec)]
    edge_loads = [
        load(2, cot_hbm.at[0], cot),
        load(3, wout_hbm, wout),
        load(4, pre_hbm.at[0], pre),
    ]
    index_loads = [
        load(5, recv_hbm, recv),
        load(6, slot_hbm, slot),
        load(7, dnode_hbm, dnode),
        load(8, hmap_hbm.at[0], hmaps.at[sec]),
    ]
    weight_load = load(9, wnode_hbm, wnode)
    for copy in first_loads:
        copy.start()

    barrier = pltpu.get_barrier_semaphore()
    for o in far_first:
        pl.semaphore_signal(barrier, inc=1, device_id=(sec, peers[o]), device_id_type=MESH)
    for other in others[1:]:
        pl.semaphore_signal(barrier, inc=1, device_id=(other, tile), device_id_type=MESH)

    for copy in edge_loads + index_loads + [weight_load]:
        copy.start()

    def over_sec(k, src, dst, send_sem, recv_sem):
        return pltpu.make_async_remote_copy(
            src_ref=src,
            dst_ref=dst,
            send_sem=send_sem.at[k - 1],
            recv_sem=recv_sem.at[k - 1],
            device_id=(others[k], tile),
            device_id_type=MESH,
        )

    def over_tile(o, quarter, src, dst, sem):
        return pltpu.make_async_remote_copy(
            src_ref=src,
            dst_ref=dst,
            send_sem=sem.at[0],
            recv_sem=sem.at[1],
            device_id=(quarter, peers[o]),
            device_id_type=MESH,
        )

    first_loads[0].wait()
    lane = iota((1, rows), 1)
    count = jnp.zeros((1, rows), jnp.int32)
    for o in range(neighbours):
        count = jnp.where(lane // capacity == o, dcnt[0:1, o : o + 1], count)
    live_lane = jnp.where(lane % capacity < count, lane // GROUP, -1)
    pick = hot(iota((groups, rows), 0) == live_lane)
    first_loads[1].wait()
    dec_out[...] = dot(pick, dec[...]).astype(BF16)

    pl.semaphore_wait(barrier, neighbours + sec_count - 1)

    for o in far_first:
        at = pl.ds(o * block, block)
        over_tile(o, sec, dec_out.at[at], dec_in.at[at], dec_sem).start()
    map_copies = [
        over_sec(k, hmap_hbm.at[0], hmaps.at[sec], map_send, map_recv)
        for k in range(1, sec_count)
    ]
    for copy in map_copies:
        copy.start()

    for copy in edge_loads:
        copy.wait()
    step = 256

    def edge_block(i, carry):
        at = pl.ds(i * step, step)
        edge_proj[at, :] = dot_nt(cot[at, :], wout[...])
        v = pre[at, :].astype(F32)
        s = jax.nn.sigmoid(v)
        slope[at, :] = s * (1.0 + v * (1.0 - s))
        return carry

    lax.fori_loop(0, edges // step, edge_block, 0)

    for copy in index_loads:
        copy.wait()
    node_row = iota((QUART, edges), 0)
    receivers = recv[...]
    edge_hot = jnp.where(node_row == receivers, F32(1.0), F32(0.0)).T.astype(BF16)
    hot_edge[:, :QUART] = edge_hot
    hot_edge[:, QUART:] = edge_hot
    live = iota((1, edges), 1) < ecnt_smem[0, 0]
    live_slot = jnp.where(live, slot[...], -1)
    live_recv = jnp.where(live, receivers, -1)
    hot_sums[0:QUART, :] = hot(node_row == live_slot - local_rows)
    for k in range(sec_count):
        hot_sums[(k + 1) * QUART : (k + 2) * QUART, :] = hot(
            node_row == live_slot - others[k] * QUART
        )
    hot_sums[(sec_count + 1) * QUART :, :] = hot(node_row == live_recv)
    first_of_group = jnp.where(lane % GROUP == 0, dnode[...], -1)
    named = hot(iota((QUART, rows), 0) == first_of_group)
    group_of = hot(iota((groups, rows), 0) == lane // GROUP)
    hot_dec[...] = dot_nt(named, group_of).astype(BF16)

    pltpu.make_async_copy(dec_in, dec_in, dec_sem.at[1]).wait()
    cot_sum = dot(hot_dec[...], dec_in[...])
    node_cot[...] = cot_sum
    high, low = split_bf16(dot_nt(cot_sum.astype(BF16), wout[...]))
    node_split[:QUART, :] = high
    node_split[QUART:, :] = low

    def delta_block(i, carry):
        at = pl.ds(i * step, step)
        act = edge_proj[at, :] + dot(hot_edge[at, :], node_split[...])
        delta[at, :] = (act * slope[at, :]).astype(BF16)
        return carry

    lax.fori_loop(0, edges // step, delta_block, 0)

    halo_rows = dot(hot_sums[0:QUART, :], delta[...]).astype(BF16)
    for j in range(sec_count):
        halo_out[j] = halo_rows[:, j * width : (j + 1) * width]
    for o in far_first:
        at = pl.ds(o * block, block)
        for j in range(sec_count):
            over_tile(o, j, halo_out.at[j, at], halo_in.at[sec, at], halo_sem).start()

    def sum_block(i, carry):
        at = pl.ds(i * QUART, QUART)
        sums[at, :] = dot(hot_sums[pl.ds((i + 1) * QUART, QUART), :], delta[...])
        return carry

    lax.fori_loop(1, sec_count, sum_block, 0)
    local_copies = [
        over_sec(k, local_out.at[k - 1], local_in.at[k - 1], local_send, local_recv)
        for k in range(1, sec_count)
    ]
    for k in range(1, sec_count):
        local_out[k - 1] = sums[k * QUART : (k + 1) * QUART, :].astype(BF16)
        local_copies[k - 1].start()
    sum_block(0, 0)
    sum_block(sec_count, 0)

    for copy in map_copies:
        copy.wait_recv()
    for k in range(sec_count):
        for q in range(sec_count):
            hot_land[k * QUART : (k + 1) * QUART, q * QUART : (q + 1) * QUART] = hot(
                iota((QUART, QUART), 0) == hmaps[q] - others[k] * QUART
            )
    weight_load.wait()
    received = split_bf16(sums[sec_count * QUART :, :])
    base[...] = (
        node_cot[...]
        + dot_nt(received[0], wnode[latent:, :])
        + dot_nt(received[1], wnode[latent:, :])
    )

    pltpu.make_async_copy(halo_in, halo_in, halo_sem.at[1]).wait()
    arrived = halo_in[...].reshape(local_rows, width)
    landed = dot(hot_land[...], arrived).astype(BF16)
    landed_copies = [
        over_sec(k, landed_out.at[k - 1], landed_in.at[sec], landed_send, landed_recv)
        for k in range(1, sec_count)
    ]
    for k in range(1, sec_count):
        landed_out[k - 1] = landed[k * QUART : (k + 1) * QUART, :]
    for copy in landed_copies:
        copy.start()
    landed_in[sec] = landed[:QUART, :]

    own = sums[:QUART, :]
    for k in range(1, sec_count):
        local_copies[k - 1].wait_recv()
        own += local_in[k - 1].astype(F32)
    sent = split_bf16(own)
    base[...] += dot_nt(sent[0], wnode[:latent, :]) + dot_nt(sent[1], wnode[:latent, :])

    for copy in landed_copies:
        copy.wait_recv()
    result = base[...]
    for j in range(sec_count):
        result += dot_nt(landed_in[j], wnode[:latent, j * width : (j + 1) * width])
    out_ref[0] = result

    for copy in map_copies + local_copies + landed_copies:
        copy.wait_send()
    pltpu.make_async_copy(dec_out, dec_out, dec_sem.at[0]).wait()
    pltpu.make_async_copy(halo_out, halo_out, halo_sem.at[0]).wait()


def per_device(
    pre_act,
    edge_cot,
    recv_local,
    send_slot,
    edge_count,
    halo_map,
    dec_rows,
    dec_count,
    dec_node,
    w_node,
    w_out,
):
    sec_count = lax.axis_size("sec")
    tile_count = lax.axis_size("tile")
    edges, latent = pre_act.shape[1:]
    rows = dec_rows.shape[1]
    neighbours = dec_count.shape[1]
    groups = rows // GROUP
    halo = halo_map.shape[2]
    width = latent // sec_count
    def hbm(x):
        return pltpu.with_memory_space_constraint(x, pltpu.HBM)

    operands = (
        hbm(pre_act),
        hbm(edge_cot),
        hbm(recv_local),
        hbm(send_slot),
        edge_count,
        hbm(halo_map),
        hbm(dec_rows),
        hbm(dec_count),
        hbm(dec_node),
        hbm(w_node),
        hbm(w_out),
    )
    vmem = pltpu.VMEM
    dma = pltpu.SemaphoreType.DMA
    return pl.pallas_call(
        functools.partial(kernel, sec_count, tile_count, neighbours),
        out_shape=vmem((1, QUART, latent), F32),
        in_specs=[
            pl.BlockSpec(memory_space=pltpu.SMEM if x is edge_count else pl.ANY) for x in operands
        ],
        out_specs=pl.BlockSpec(memory_space=vmem),
        scratch_shapes=[
            vmem((edges, latent), BF16),
            vmem((edges, latent), BF16),
            vmem((1, edges), jnp.int32),
            vmem((1, edges), jnp.int32),
            vmem((sec_count, 1, halo), jnp.int32),
            vmem((rows, latent), BF16),
            vmem((1, neighbours), jnp.int32),
            vmem((1, rows), jnp.int32),
            vmem(w_node.shape, BF16),
            vmem(w_out.shape, BF16),
            vmem((edges, latent), F32),
            vmem((edges, latent), F32),
            vmem((edges, latent), BF16),
            vmem((edges, 2 * QUART), BF16),
            vmem(((sec_count + 2) * QUART, edges), BF16),
            vmem((QUART, groups), BF16),
            vmem((sec_count * QUART, sec_count * halo), BF16),
            vmem((2 * QUART, latent), BF16),
            vmem((QUART, latent), F32),
            vmem((QUART, latent), F32),
            vmem(((sec_count + 1) * QUART, latent), F32),
            vmem((groups, latent), BF16),
            vmem((groups, latent), BF16),
            vmem((sec_count, halo, width), BF16),
            vmem((sec_count, halo, width), BF16),
            vmem((sec_count - 1, QUART, latent), BF16),
            vmem((sec_count - 1, QUART, latent), BF16),
            vmem((sec_count - 1, QUART, width), BF16),
            vmem((sec_count, QUART, width), BF16),
            dma((10,)),
            dma((sec_count - 1,)),
            dma((sec_count - 1,)),
            dma((2,)),
            dma((2,)),
            dma((sec_count - 1,)),
            dma((sec_count - 1,)),
            dma((sec_count - 1,)),
            dma((sec_count - 1,)),
        ],
        compiler_params=pltpu.CompilerParams(
            collective_id=0, has_side_effects=True, vmem_limit_bytes=40 * 1024 * 1024
        ),
        cost_estimate=pl.CostEstimate(
            flops=2 * 1000 * 1000 * 1000, bytes_accessed=4 * 1024 * 1024, transcendentals=0
        ),
    )(*operands)


def solution(mesh):
    return jax.shard_map(
        per_device,
        mesh=mesh,
        in_specs=(
            P("sec", "tile", None),
            P("sec", "tile", None),
            P("sec", "tile"),
            P("sec", "tile"),
            P("sec", "tile"),
            P("sec", "tile", None),
            P("sec", "tile", None),
            P("sec", "tile"),
            P("sec", "tile"),
            P(),
            P(),
        ),
        out_specs=P("sec", "tile", None),
        check_vma=False,
    )
```

time: 37.4 us -> 33.1 us (0.89); the launches traced: 36.6 us -> 33 us
  Pallas kernels: 34.3 us -> 31.6 us
  local copies, waits for them, and re-layouts: 1.67 us -> 0.71 us
    pallas_call x1, Pallas kernels: 34.3 us -> 31.6 us  [per_device(): pl.pallas_call(functools.partial(kernel, sec_count, tile_count, neighbour...]
    unnamed x1, local copies, waits for them, and re-layouts: 1.67 us -> 0.71 us
where the time goes in v2:
time: 33.1 us; the launch traced here: 33 us
  Pallas kernels  31.6 us (95%)
  local copies, waits for them, and re-layouts  0.71 us (2%)
  between operations  0.66 us (2%)
    pallas_call x1, Pallas kernels, per_device(): pl.pallas_call(functools.partial(kernel, sec_count, tile_count, neighbour...  31.6 us
    unnamed x1, local copies, waits for them, and re-layouts  0.71 us

profile of v2, /device:TPU:1, one launch (start us, length us, event | category | flops | bytes accessed | tf_op | source)
XLA Modules:
  0.0 33.0 jit_solution(5157174368239150825)
XLA Ops:
  0.7 31.6 %shard_map.109 = f32[1,128,512]{2,1,0:T(8,128)S(1)} custom-call(bf16[1,1024,512]{2,1,0:T(8,128)(2,1)} %pre_hbm.1, bf16[1,1024,512]{2,1,0:T(8,128)(2,1)} %cot_hbm.1, s32[1,1024]{1,0:T(1,128)} %recv_hbm.1, s32[1,1024]{1,0:T(1,128)} %slot_hbm.1, s32[1,1]{1,0:T(1,128)S(6)} %copy.14.ecnt_smem, s32[1,1,128]{2,1,0:T(1,128)} %hmap_hbm.1, ...), custom_call_target="tpu_custom_call" | custom-call | flops 2000000000 | bytes 4194304 | tf_op jit(solution)/shard_map/pallas_call | solution.py:346
  32.3 0.7 %copy.13 = f32[1,128,512]{2,1,0:T(8,128)} copy(f32[1,128,512]{2,1,0:T(8,128)S(1)} %shard_map.109) | data formatting | bytes 524288

commit v3 on v2

--- a/solution.py
+++ b/solution.py
@@ -10,6 +10,7 @@
 MESH = pl.DeviceIdType.MESH
 QUART = 128
 GROUP = 4
+PAIR = 4
 NT = (((1,), (1,)), ((), ()))
 F32 = jnp.float32
 BF16 = jnp.bfloat16
@@ -101,7 +102,7 @@
     groups = dec_in.shape[0]
     block = groups // neighbours
     capacity = rows // neighbours
-    width = latent // sec_count
+    width = latent // PAIR
     local_rows = sec_count * QUART
     sec = lax.axis_index("sec")
     tile = lax.axis_index("tile")
@@ -111,6 +112,13 @@
         for o in range(neighbours)
     ]
     far_first = sorted(range(neighbours), key=lambda o: -abs(offset_value(o, neighbours)))
+
+    far_pairs = sorted(
+        ((o, k) for o in range(neighbours) for k in range(sec_count)),
+        key=lambda pair: -(
+            abs(offset_value(pair[0], neighbours)) / 2 + min(pair[1], sec_count - pair[1])
+        ),
+    )
 
     def load(i, src, dst):
         return pltpu.make_async_copy(src, dst, load_sem.at[i])
@@ -230,15 +238,16 @@
         delta[at, :] = (act * slope[at, :]).astype(BF16)
         return carry
 
-    lax.fori_loop(0, edges // step, delta_block, 0)
+    lax.fori_loop(0, edges // step, delta_block, 0, unroll=True)
 
     halo_rows = dot(hot_sums[0:QUART, :], delta[...]).astype(BF16)
-    for j in range(sec_count):
+    for j in range(PAIR):
         halo_out[j] = halo_rows[:, j * width : (j + 1) * width]
-    for o in far_first:
+    for o, k in far_pairs:
         at = pl.ds(o * block, block)
-        for j in range(sec_count):
-            over_tile(o, j, halo_out.at[j, at], halo_in.at[sec, at], halo_sem).start()
+        over_tile(
+            o, others[k], halo_out.at[others[k], at], halo_in.at[sec, at], halo_sem
+        ).start()
 
     def sum_block(i, carry):
         at = pl.ds(i * QUART, QUART)
@@ -259,7 +268,7 @@
     for copy in map_copies:
         copy.wait_recv()
     for k in range(sec_count):
-        for q in range(sec_count):
+        for q in range(PAIR):
             hot_land[k * QUART : (k + 1) * QUART, q * QUART : (q + 1) * QUART] = hot(
                 iota((QUART, QUART), 0) == hmaps[q] - others[k] * QUART
             )
@@ -272,7 +281,7 @@
     )
 
     pltpu.make_async_copy(halo_in, halo_in, halo_sem.at[1]).wait()
-    arrived = halo_in[...].reshape(local_rows, width)
+    arrived = halo_in[...].reshape(PAIR * QUART, width)
     landed = dot(hot_land[...], arrived).astype(BF16)
     landed_copies = [
         over_sec(k, landed_out.at[k - 1], landed_in.at[sec], landed_send, landed_recv)
@@ -284,19 +293,18 @@
         copy.start()
     landed_in[sec] = landed[:QUART, :]
 
-    own = sums[:QUART, :]
+    total = sums[:QUART, :]
     for k in range(1, sec_count):
         local_copies[k - 1].wait_recv()
-        own += local_in[k - 1].astype(F32)
-    sent = split_bf16(own)
+        total += local_in[k - 1].astype(F32)
+    sent = split_bf16(total)
     base[...] += dot_nt(sent[0], wnode[:latent, :]) + dot_nt(sent[1], wnode[:latent, :])
 
     for copy in landed_copies:
         copy.wait_recv()
-    result = base[...]
-    for j in range(sec_count):
-        result += dot_nt(landed_in[j], wnode[:latent, j * width : (j + 1) * width])
-    out_ref[0] = result
+    columns = jnp.concatenate([landed_in[j] for j in range(sec_count)], axis=1)
+    weights = jnp.concatenate([wnode[:latent, :]] * (sec_count // PAIR), axis=1)
+    out_ref[0] = base[...] + dot_nt(columns, weights)
 
     for copy in map_copies + local_copies + landed_copies:
         copy.wait_send()
@@ -324,7 +332,7 @@
     neighbours = dec_count.shape[1]
     groups = rows // GROUP
     halo = halo_map.shape[2]
-    width = latent // sec_count
+    width = latent // PAIR
     def hbm(x):
         return pltpu.with_memory_space_constraint(x, pltpu.HBM)
 
@@ -355,7 +363,7 @@
             vmem((edges, latent), BF16),
             vmem((1, edges), jnp.int32),
             vmem((1, edges), jnp.int32),
-            vmem((sec_count, 1, halo), jnp.int32),
+            vmem((PAIR, 1, halo), jnp.int32),
             vmem((rows, latent), BF16),
             vmem((1, neighbours), jnp.int32),
             vmem((1, rows), jnp.int32),
@@ -367,15 +375,15 @@
             vmem((edges, 2 * QUART), BF16),
             vmem(((sec_count + 2) * QUART, edges), BF16),
             vmem((QUART, groups), BF16),
-            vmem((sec_count * QUART, sec_count * halo), BF16),
+            vmem((sec_count * QUART, PAIR * halo), BF16),
             vmem((2 * QUART, latent), BF16),
             vmem((QUART, latent), F32),
             vmem((QUART, latent), F32),
             vmem(((sec_count + 1) * QUART, latent), F32),
             vmem((groups, latent), BF16),
             vmem((groups, latent), BF16),
-            vmem((sec_count, halo, width), BF16),
-            vmem((sec_count, halo, width), BF16),
+            vmem((PAIR, halo, width), BF16),
+            vmem((PAIR, halo, width), BF16),
             vmem((sec_count - 1, QUART, latent), BF16),
             vmem((sec_count - 1, QUART, latent), BF16),
             vmem((sec_count - 1, QUART, width), BF16),

time: 33.1 us -> 32.4 us (0.979)
  Pallas kernels: 31.6 us -> 30.9 us
    pallas_call x1, Pallas kernels: 31.6 us -> 30.9 us  [per_device(): pl.pallas_call(functools.partial(kernel, sec_count, tile_count, neighbour...]
where the time goes in v3:
time: 32.4 us; the launch traced here: 32.3 us
  Pallas kernels  30.9 us (95%)
  local copies, waits for them, and re-layouts  0.71 us (2%)
  between operations  0.66 us (2%)
    pallas_call x1, Pallas kernels, per_device(): pl.pallas_call(functools.partial(kernel, sec_count, tile_count, neighbour...  30.9 us
    unnamed x1, local copies, waits for them, and re-layouts  0.71 us

profile of v3, /device:TPU:1, one launch (start us, length us, event | category | flops | bytes accessed | tf_op | source)
XLA Modules:
  0.0 32.3 jit_solution(4400208633297416047)
XLA Ops:
  0.7 30.9 %shard_map.109 = f32[1,128,512]{2,1,0:T(8,128)S(1)} custom-call(bf16[1,1024,512]{2,1,0:T(8,128)(2,1)} %pre_hbm.1, bf16[1,1024,512]{2,1,0:T(8,128)(2,1)} %cot_hbm.1, s32[1,1024]{1,0:T(1,128)} %recv_hbm.1, s32[1,1024]{1,0:T(1,128)} %slot_hbm.1, s32[1,1]{1,0:T(1,128)S(6)} %copy.14.ecnt_smem, s32[1,1,128]{2,1,0:T(1,128)} %hmap_hbm.1, ...), custom_call_target="tpu_custom_call" | custom-call | flops 2000000000 | bytes 4194304 | tf_op jit(solution)/shard_map/pallas_call | solution.py:354
  31.6 0.7 %copy.13 = f32[1,128,512]{2,1,0:T(8,128)} copy(f32[1,128,512]{2,1,0:T(8,128)S(1)} %shard_map.109) | data formatting | bytes 524288

commit v4 on v3

--- a/solution.py
+++ b/solution.py
@@ -68,6 +68,8 @@
     dnode,
     wnode,
     wout,
+    wout_t,
+    wsend_t,
     edge_proj,
     slope,
     delta,
@@ -204,6 +206,7 @@
 
     lax.fori_loop(0, edges // step, edge_block, 0)
 
+    wout_t[...] = wout[...].astype(F32).T.astype(BF16)
     for copy in index_loads:
         copy.wait()
     node_row = iota((QUART, edges), 0)
@@ -228,7 +231,7 @@
     pltpu.make_async_copy(dec_in, dec_in, dec_sem.at[1]).wait()
     cot_sum = dot(hot_dec[...], dec_in[...])
     node_cot[...] = cot_sum
-    high, low = split_bf16(dot_nt(cot_sum.astype(BF16), wout[...]))
+    high, low = split_bf16(dot(cot_sum.astype(BF16), wout_t[...]))
     node_split[:QUART, :] = high
     node_split[QUART:, :] = low
 
@@ -273,6 +276,7 @@
                 iota((QUART, QUART), 0) == hmaps[q] - others[k] * QUART
             )
     weight_load.wait()
+    wsend_t[...] = wnode[:latent, :].astype(F32).T.astype(BF16)
     received = split_bf16(sums[sec_count * QUART :, :])
     base[...] = (
         node_cot[...]
@@ -303,8 +307,7 @@
     for copy in landed_copies:
         copy.wait_recv()
     columns = jnp.concatenate([landed_in[j] for j in range(sec_count)], axis=1)
-    weights = jnp.concatenate([wnode[:latent, :]] * (sec_count // PAIR), axis=1)
-    out_ref[0] = base[...] + dot_nt(columns, weights)
+    out_ref[0] = base[...] + dot(columns, wsend_t[...])
 
     for copy in map_copies + local_copies + landed_copies:
         copy.wait_send()
@@ -369,6 +372,8 @@
             vmem((1, rows), jnp.int32),
             vmem(w_node.shape, BF16),
             vmem(w_out.shape, BF16),
+            vmem((latent, latent), BF16),
+            vmem((latent, latent), BF16),
             vmem((edges, latent), F32),
             vmem((edges, latent), F32),
             vmem((edges, latent), BF16),

time: 32.4 us -> 32.3 us (level)
  no operation moved by 1% of the time
where the time goes in v4:
time: 32.3 us; the launch traced here: 32.2 us
  Pallas kernels  30.8 us (95%)
  local copies, waits for them, and re-layouts  0.71 us (2%)
  between operations  0.66 us (2%)
    pallas_call x1, Pallas kernels, per_device(): pl.pallas_call(functools.partial(kernel, sec_count, tile_count, neighbour...  30.8 us
    unnamed x1, local copies, waits for them, and re-layouts  0.71 us

profile of v4, /device:TPU:1, one launch (start us, length us, event | category | flops | bytes accessed | tf_op | source)
XLA Modules:
  0.0 32.2 jit_solution(13117707689714277627)
XLA Ops:
  0.7 30.8 %shard_map.109 = f32[1,128,512]{2,1,0:T(8,128)S(1)} custom-call(bf16[1,1024,512]{2,1,0:T(8,128)(2,1)} %pre_hbm.1, bf16[1,1024,512]{2,1,0:T(8,128)(2,1)} %cot_hbm.1, s32[1,1024]{1,0:T(1,128)} %recv_hbm.1, s32[1,1024]{1,0:T(1,128)} %slot_hbm.1, s32[1,1]{1,0:T(1,128)S(6)} %copy.14.ecnt_smem, s32[1,1,128]{2,1,0:T(1,128)} %hmap_hbm.1, ...), custom_call_target="tpu_custom_call" | custom-call | flops 2000000000 | bytes 4194304 | tf_op jit(solution)/shard_map/pallas_call | solution.py:357
  31.5 0.7 %copy.13 = f32[1,128,512]{2,1,0:T(8,128)} copy(f32[1,128,512]{2,1,0:T(8,128)S(1)} %shard_map.109) | data formatting | bytes 524288

commit v5 on v3

--- a/solution.py
+++ b/solution.py
@@ -183,13 +183,6 @@
     for o in far_first:
         at = pl.ds(o * block, block)
         over_tile(o, sec, dec_out.at[at], dec_in.at[at], dec_sem).start()
-    map_copies = [
-        over_sec(k, hmap_hbm.at[0], hmaps.at[sec], map_send, map_recv)
-        for k in range(1, sec_count)
-    ]
-    for copy in map_copies:
-        copy.start()
-
     for copy in edge_loads:
         copy.wait()
     step = 256
@@ -202,8 +195,14 @@
         slope[at, :] = s * (1.0 + v * (1.0 - s))
         return carry
 
-    lax.fori_loop(0, edges // step, edge_block, 0)
-
+    lax.fori_loop(0, edges // step, edge_block, 0, unroll=True)
+
+    map_copies = [
+        over_sec(k, hmap_hbm.at[0], hmaps.at[sec], map_send, map_recv)
+        for k in range(1, sec_count)
+    ]
+    for copy in map_copies:
+        copy.start()
     for copy in index_loads:
         copy.wait()
     node_row = iota((QUART, edges), 0)
@@ -254,7 +253,7 @@
         sums[at, :] = dot(hot_sums[pl.ds((i + 1) * QUART, QUART), :], delta[...])
         return carry
 
-    lax.fori_loop(1, sec_count, sum_block, 0)
+    lax.fori_loop(1, sec_count, sum_block, 0, unroll=True)
     local_copies = [
         over_sec(k, local_out.at[k - 1], local_in.at[k - 1], local_send, local_recv)
         for k in range(1, sec_count)

time: 32.4 us -> 32.4 us (level)
  no operation moved by 1% of the time
where the time goes in v5:
time: 32.4 us; the launch traced here: 32.3 us
  Pallas kernels  30.9 us (95%)
  local copies, waits for them, and re-layouts  0.71 us (2%)
  between operations  0.66 us (2%)
    pallas_call x1, Pallas kernels, per_device(): pl.pallas_call(functools.partial(kernel, sec_count, tile_count, neighbour...  30.9 us
    unnamed x1, local copies, waits for them, and re-layouts  0.71 us

profile of v5, /device:TPU:1, one launch (start us, length us, event | category | flops | bytes accessed | tf_op | source)
XLA Modules:
  0.0 32.3 jit_solution(2025179311579079323)
XLA Ops:
  0.7 30.9 %shard_map.109 = f32[1,128,512]{2,1,0:T(8,128)S(1)} custom-call(bf16[1,1024,512]{2,1,0:T(8,128)(2,1)} %pre_hbm.1, bf16[1,1024,512]{2,1,0:T(8,128)(2,1)} %cot_hbm.1, s32[1,1024]{1,0:T(1,128)} %recv_hbm.1, s32[1,1024]{1,0:T(1,128)} %slot_hbm.1, s32[1,1]{1,0:T(1,128)S(6)} %copy.14.ecnt_smem, s32[1,1,128]{2,1,0:T(1,128)} %hmap_hbm.1, ...), custom_call_target="tpu_custom_call" | custom-call | flops 2000000000 | bytes 4194304 | tf_op jit(solution)/shard_map/pallas_call | solution.py:353
  31.5 0.7 %copy.13 = f32[1,128,512]{2,1,0:T(8,128)} copy(f32[1,128,512]{2,1,0:T(8,128)S(1)} %shard_map.109) | data formatting | bytes 524288
